TPU v7x, 32 devices: a whole 2x2x4 slice. The times are simulated.
32 devices in a mesh: blk: 8 (over z, x), group: 4 (over y, core).
Axes of the slice: x: 2, y: 2, z: 4, core: 2. Of those that a mesh axis runs over, the one named last changes fastest.
Arguments:
- queries: bfloat16 [8, 2048, 2560], P('blk', 'group'), may hold values from -6 to 6
- new_keys: bfloat16 [8, 2048, 256], P('blk', 'group'), may hold values from -15 to 15
- new_values: bfloat16 [8, 2048, 256], P('blk', 'group'), may hold values from -4 to 4
- key_cache: bfloat16 [320, 128, 256], P('blk', 'group'), may hold values from -4 to 4
- value_cache: bfloat16 [320, 128, 256], P('blk', 'group'), may hold values from -4 to 4
- out_weight: bfloat16 [2560, 2560], replicated, may hold values from -0.375 to 0.375
- lengths: int32 [8], replicated, may hold values from 0 to 30720, as said below
- page_table: int32 [8, 32], replicated, may hold values from 0 to 319, as said below
Outputs:
- hidden_states: bfloat16 [8, 2048, 2560], P('blk', 'group')
- key_cache_out: bfloat16 [320, 128, 256], P('blk', 'group')
- value_cache_out: bfloat16 [320, 128, 256], P('blk', 'group')
Inputs may be any that keep to these rules, and one draw needn't show every extreme that they name: `lengths`: multiples of 2048; some request has length 0 and some has 30720. `page_table`: all entries differ; page p lies on blk index p // 40; columns below 16 hold the request's last 16 pages before its group in order (pages that hold no part of a request where its length is short), the others the pages of its group in order; of one request's first 16 entries at most 2 lie on one blk index, of its last 16 at most 2, and both bounds are reached for every request.
All inputs are finite; a program needn't handle non-finite values.
Results may differ from a plain program's by a relative error of at most 0.009.
Values may be sent and summed in bfloat16 or wider, within the bound.
No kernel may reach another device: no remote copies, remote signals or barrier semaphores. Data moves between devices by JAX's collectives and lax.ppermute only.
A program may use at most 256 MiB of HBM per device.

v0:
```python
import jax
import jax.numpy as jnp
from jax import lax
from jax.sharding import PartitionSpec as P

masked_score = -1e30
key_block_size = 512


def rotate(values, positions):
    quarter = values.shape[-1] // 4
    freq_table = 10000.0 ** (-jnp.arange(quarter, dtype=jnp.float32) / quarter)
    angles = positions.astype(jnp.float32)[..., None] * freq_table
    cosine = jnp.cos(angles)
    sine_part = jnp.sin(angles)
    leading = values[..., :quarter]
    trailing = values[..., quarter : 2 * quarter]
    return jnp.concatenate(
        [
            leading * cosine - trailing * sine_part,
            trailing * cosine + leading * sine_part,
            values[..., 2 * quarter :],
        ],
        axis=-1,
    )


def attend_block(carried, query_block, key_rows, value_rows, visible, score_scale):
    running_max, running_sum, running_acc = carried
    scores = (
        jnp.einsum("thd,kd->thk", query_block, key_rows, preferred_element_type=jnp.float32)
        * score_scale
    )
    scores = jnp.where(visible, scores, masked_score)
    new_max = jnp.maximum(running_max, jnp.max(scores, axis=2))
    weights = jnp.where(visible, jnp.exp(scores - new_max[:, :, None]), 0.0)
    factor = jnp.exp(running_max - new_max)
    new_sum = running_sum * factor + jnp.sum(weights, axis=2)
    new_acc = running_acc * factor[:, :, None] + jnp.einsum(
        "thk,kd->thd", weights.astype(jnp.bfloat16), value_rows, preferred_element_type=jnp.float32
    )
    return (new_max, new_sum, new_acc)


def attend(carried, query_block, key_rows, value_rows, visible, score_scale):
    key_total = key_rows.shape[0]
    for block_start in range(0, key_total, key_block_size):
        block_stop = min(block_start + key_block_size, key_total)
        carried = attend_block(
            carried,
            query_block,
            key_rows[block_start:block_stop],
            value_rows[block_start:block_stop],
            visible[:, :, block_start:block_stop],
            score_scale,
        )
    return carried


def body(queries, new_keys, new_values, key_cache, value_cache, out_weight, lengths, page_table):
    blk_count = lax.axis_size("blk")
    blk_index = lax.axis_index("blk")
    group_count = lax.axis_size("group")
    group_index = lax.axis_index("group")
    tok_rows = queries.shape[1]
    head_dim = new_keys.shape[2]
    head_count = queries.shape[2] // head_dim
    pages_here = key_cache.shape[0]
    page_rows = key_cache.shape[1]
    page_len = page_rows * group_count
    slot_count = page_table.shape[1]
    group_len = tok_rows * group_count
    fresh_pages = group_len // page_len
    window_pages = slot_count - fresh_pages
    window_len = window_pages * page_len
    score_scale = head_dim ** (-0.5)
    length = lengths[blk_index]
    my_table = page_table[blk_index]
    offsets = group_index * tok_rows + jnp.arange(tok_rows, dtype=jnp.int32)
    positions = length + offsets
    roped_queries = rotate(
        queries[0].astype(jnp.float32).reshape(tok_rows, head_count, head_dim), positions[:, None]
    ).astype(jnp.bfloat16)
    roped_keys = rotate(new_keys[0].astype(jnp.float32), positions).astype(jnp.bfloat16)
    all_keys, all_values = (
        lax.all_gather(roped_keys, "group", axis=0, tiled=True),
        lax.all_gather(new_values[0], "group", axis=0, tiled=True),
    )
    key_index = jnp.arange(group_len, dtype=jnp.int32)
    fresh_visible = key_index[None, :] <= offsets[:, None]
    initial = (
        jnp.full((tok_rows, head_count), masked_score, jnp.float32),
        jnp.zeros((tok_rows, head_count), jnp.float32),
        jnp.zeros((tok_rows, head_count, head_dim), jnp.float32),
    )
    carried = attend(
        initial, roped_queries, all_keys, all_values, fresh_visible[:, None, :], score_scale
    )
    old_table = my_table[:window_pages]
    blank_pages = jnp.zeros((window_pages, page_rows, head_dim), jnp.bfloat16)
    pieces = (
        lax.all_gather(key_cache, "blk", axis=0, tiled=True),
        lax.all_gather(value_cache, "blk", axis=0, tiled=True),
    )
    held_pages = pieces[0].shape[0]
    inside = (old_table >= 0) & (old_table < held_pages)
    clipped = jnp.clip(old_table, 0, held_pages - 1)
    old_keys = jnp.where(inside[:, None, None], pieces[0][clipped], blank_pages)
    old_values = jnp.where(inside[:, None, None], pieces[1][clipped], blank_pages)
    pieces = (
        lax.all_gather(old_keys, "group", axis=1, tiled=True),
        lax.all_gather(old_values, "group", axis=1, tiled=True),
    )
    piece_rows = pieces[0].shape[1]
    key_rows = pieces[0].reshape(-1, head_dim)
    value_rows = pieces[1].reshape(-1, head_dim)
    in_window = (
        jnp.arange(window_pages, dtype=jnp.int32)[:, None] * page_len
        + jnp.arange(piece_rows, dtype=jnp.int32)[None, :]
    ).reshape(-1)
    visible = (in_window[None, :] > offsets[:, None]) & (
        length - window_len + in_window[None, :] >= 0
    )
    carried = attend(carried, roped_queries, key_rows, value_rows, visible[:, None, :], score_scale)
    running_max, running_sum, running_acc = carried
    attended = (
        (running_acc / running_sum[:, :, None])
        .astype(jnp.bfloat16)
        .reshape(tok_rows, head_count * head_dim)
    )
    hidden = jnp.dot(attended, out_weight, preferred_element_type=jnp.float32).astype(jnp.bfloat16)[
        None
    ]
    cap_new = (fresh_pages + blk_count - 1) // blk_count
    quarter_keys = lax.dynamic_index_in_dim(
        all_keys.reshape(fresh_pages, group_count, page_rows, head_dim),
        group_index,
        axis=1,
        keepdims=False,
    )
    quarter_values = lax.dynamic_index_in_dim(
        all_values.reshape(fresh_pages, group_count, page_rows, head_dim),
        group_index,
        axis=1,
        keepdims=False,
    )
    new_owner = my_table[window_pages:] // pages_here
    fresh_ids = jnp.arange(fresh_pages, dtype=jnp.int32)
    before = fresh_ids[None, :] < fresh_ids[:, None]
    new_rank = jnp.sum(
        (before & (new_owner[None, :] == new_owner[:, None])).astype(jnp.int32), axis=1
    )
    placing = (
        (new_owner[None, None, :] == jnp.arange(blk_count, dtype=jnp.int32)[:, None, None])
        & (new_rank[None, None, :] == jnp.arange(cap_new, dtype=jnp.int32)[None, :, None])
    ).astype(jnp.bfloat16)
    send_new_keys = jnp.einsum(
        "ocj,jrd->ocrd", placing, quarter_keys, preferred_element_type=jnp.float32
    ).astype(jnp.bfloat16)
    send_new_values = jnp.einsum(
        "ocj,jrd->ocrd", placing, quarter_values, preferred_element_type=jnp.float32
    ).astype(jnp.bfloat16)
    arrived_keys, arrived_values = (
        lax.all_to_all(send_new_keys, "blk", split_axis=0, concat_axis=0, tiled=True),
        lax.all_to_all(send_new_values, "blk", split_axis=0, concat_axis=0, tiled=True),
    )
    owned_slots = page_table[:, window_pages:] // pages_here == blk_index
    hit_rank = jnp.cumsum(owned_slots.astype(jnp.int32), axis=1) - 1
    choose = owned_slots[:, None, :] & (
        hit_rank[:, None, :] == jnp.arange(cap_new, dtype=jnp.int32)[None, :, None]
    )
    target = jnp.where(
        jnp.any(choose, axis=2),
        jnp.sum(jnp.where(choose, page_table[:, None, window_pages:] % pages_here, 0), axis=2),
        pages_here,
    )
    key_out = key_cache.at[target.reshape(-1)].set(
        arrived_keys.reshape(-1, page_rows, head_dim), mode="drop"
    )
    value_out = value_cache.at[target.reshape(-1)].set(
        arrived_values.reshape(-1, page_rows, head_dim), mode="drop"
    )
    return (hidden, key_out, value_out)


def solution(mesh):
    return jax.shard_map(
        body,
        mesh=mesh,
        in_specs=(
            P("blk", "group", None),
            P("blk", "group", None),
            P("blk", "group", None),
            P("blk", "group", None),
            P("blk", "group", None),
            P(),
            P(),
            P(),
        ),
        out_specs=(P("blk", "group", None), P("blk", "group", None), P("blk", "group", None)),
        check_vma=False,
    )
```

profile of v0, /device:TPU:0, one launch (start us, length us, event | category | flops | bytes accessed | tf_op | source)
XLA Modules:
  0.0 423.9 jit_solution(5386290467370785093)
XLA Ops:
  7.2 2.0 copy.115
  9.2 2.0 copy.116
  11.2 1.0 bitcast_convert_fusion
  12.1 0.9 slice.183
  13.1 1.3 dynamic_slice.13
  14.4 0.7 add_convert_fusion.2
  15.1 1.2 subtract_convert_fusion.1
  16.3 0.9 pad_maximum_fusion.1
  17.3 1.8 copy.71
  19.1 0.7 all-gather.10.cloned.1.call-update
  20.4 4.4 %copy.68 = bf16[1,512,2560]{1,2,0:T(8,128)(2,1)} copy(bf16[1,512,2560]{2,1,0:T(8,128)(2,1)} %param.8) | data formatting | bytes 5242880 | tf_op args[0]
  24.8 3.0 copy.69
  27.8 1.3 slice.180
  29.1 2.8 convert_element_type.73
  33.8 3.5 subtract_convert_fusion
  37.3 2.5 pad_maximum_fusion
  40.0 2.2 iota_compare_fusion
  42.2 1.1 slice_bitcast_fusion.7
  43.2 1.2 slice_bitcast_fusion.3
  44.4 1.0 constant_dynamic-slice_fusion
  45.7 0.8 copy.86
  46.4 7.2 %all-to-all-start = ((bf16[8,2,32,256]{3,2,1,0:T(8,128)(2,1)}), bf16[8,2,32,256]{3,2,1,0:T(8,128)(2,1)S(1)}, u32[]{:S(2)}, u32[]{:S(2)}) async-start(bf16[8,2,32,256]{3,2,1,0:T(8,128)(2,1)} %copy.86), calls=%async_computation | async-start | bytes 524288 | tf_op jit(solution)/shard_map/all_to_all | solution.py:164
  54.0 1.2 all-gather.18.cloned.1.call-done
  55.2 2.3 copy.87
  57.4 1.0 constant_dynamic-slice_fusion.1
  58.7 0.8 copy.89
  59.4 7.3 %fusion.3 = (f32[512,10]{0,1:T(8,128)}, f32[512,10,512]{0,2,1:T(8,128)}) fusion(pred[512,512]{0,1:T(8,128)(4,1)S(1)} %get-tuple-element.29, bf16[512,10,256]{2,0,1:T(8,128)(2,1)S(1)} %pad_maximum_fusion, bf16[2048,256]{1,0:T(8,128)(2,1)} %all-gather.8.cloned.1.call-done), kind=kOutput, calls=%fused_computation.23 | convolution fusion | flops 1350036480 | bytes 13651968 | tf_op jit(solution)/shard_map/thd,kd->thk/dot_general | solution.py:31
  66.7 77.5 %all-gather.10.cloned.1.call-done = bf16[320,32,256]{2,1,0:T(8,128)(2,1)} async-done(((bf16[40,32,256]{2,1,0:T(8,128)(2,1)}), bf16[320,32,256]{2,1,0:T(8,128)(2,1)}) %all-gather.10.cloned.1.call-update) | async-done | bytes 5242896 | tf_op jit(solution)/shard_map/all_gather | solution.py:102
  144.2 3.0 gather_fusion
  147.3 83.5 %all-gather.14.cloned.1.call-done = bf16[320,32,256]{2,1,0:T(8,128)(2,1)} async-done(((bf16[40,32,256]{2,1,0:T(8,128)(2,1)}), bf16[320,32,256]{2,1,0:T(8,128)(2,1)}) %all-gather.14.cloned.1.call-update) | async-done | bytes 5242896 | tf_op jit(solution)/shard_map/all_gather | solution.py:103
  230.7 3.0 gather_fusion.1
  233.8 0.9 broadcast_select_fusion.1
  234.7 7.5 %fusion.2 = (f32[512,10]{0,1:T(8,128)}, f32[512,10,512]{0,2,1:T(8,128)}) fusion(pred[512,512]{0,1:T(8,128)(4,1)} %get-tuple-element.30, bf16[512,10,256]{2,0,1:T(8,128)(2,1)S(1)} %pad_maximum_fusion, bf16[2048,256]{1,0:T(8,128)(2,1)} %all-gather.8.cloned.1.call-done), kind=kOutput, calls=%fused_computation.22 | convolution fusion | flops 1350036480 | bytes 13651968 | tf_op jit(solution)/shard_map/thd,kd->thk/dot_general | solution.py:31
  242.2 7.2 %fusion.1 = (f32[512,10]{0,1:T(8,128)}, f32[512,10,512]{0,2,1:T(8,128)}) fusion(pred[512,512]{0,1:T(8,128)(4,1)S(1)} %copy-done.9, bf16[512,10,256]{2,0,1:T(8,128)(2,1)S(1)} %pad_maximum_fusion, bf16[2048,256]{1,0:T(8,128)(2,1)} %all-gather.8.cloned.1.call-done), kind=kOutput, calls=%fused_computation.21 | convolution fusion | flops 1350036480 | bytes 13651968 | tf_op jit(solution)/shard_map/thd,kd->thk/dot_general | solution.py:31
  249.4 3.6 all-to-all-start.1
  253.1 7.5 %fusion = (f32[512,10]{0,1:T(8,128)S(1)}, f32[512,10,512]{0,2,1:T(8,128)}) fusion(pred[512,512]{0,1:T(8,128)(4,1)} %get-tuple-element.28, bf16[512,10,256]{2,0,1:T(8,128)(2,1)} %copy-done.5, bf16[2048,256]{1,0:T(8,128)(2,1)} %all-gather.8.cloned.1.call-done), kind=kOutput, calls=%fused_computation.20 | convolution fusion | flops 1350036480 | bytes 13651968 | tf_op jit(solution)/shard_map/thd,kd->thk/dot_general | solution.py:31
  260.5 1.0 scatter_fusion
  261.6 1.6 scatter_fusion.1
  263.3 1.5 fusion.137
  264.8 7.5 %fusion.4 = (f32[512,10]{0,1:T(8,128)S(1)}, f32[512,10,512]{0,2,1:T(8,128)}) fusion(pred[512,512]{0,1:T(8,128)(4,1)S(1)} %copy-done.14, bf16[512,10,256]{2,0,1:T(8,128)(2,1)} %copy-done.5, bf16[512,256,1]{1,0,2:T(8,128)(2,1)S(1)} %bitcast.165), kind=kOutput, calls=%fused_computation.24 | convolution fusion | flops 1350036480 | bytes 13651968 | tf_op jit(solution)/shard_map/thd,kd->thk/dot_general | solution.py:31
  272.3 5.8 %fusion.5 = (f32[512,10]{0,1:T(8,128)S(1)}, f32[512,10,512]{0,2,1:T(8,128)}) fusion(pred[512,512]{0,1:T(8,128)(4,1)S(1)} %copy-done.16, bf16[512,10,256]{2,0,1:T(8,128)(2,1)S(1)} %copy-done.6, bf16[512,256,1]{1,0,2:T(8,128)(2,1)S(1)} %bitcast.164), kind=kOutput, calls=%fused_computation.25 | convolution fusion | flops 1350036480 | bytes 13651968 | tf_op jit(solution)/shard_map/thd,kd->thk/dot_general | solution.py:31
  278.0 5.8 %fusion.6 = (f32[512,10]{0,1:T(8,128)S(1)}, f32[512,10,512]{0,2,1:T(8,128)}) fusion(pred[512,512]{0,1:T(8,128)(4,1)S(1)} %copy-done.17, bf16[512,10,256]{2,0,1:T(8,128)(2,1)S(1)} %copy-done.6, bf16[512,256,1]{1,0,2:T(8,128)(2,1)S(1)} %bitcast.162), kind=kOutput, calls=%fused_computation.26 | convolution fusion | flops 1350036480 | bytes 13651968 | tf_op jit(solution)/shard_map/thd,kd->thk/dot_general | solution.py:31
  283.9 1.9 fusion.7
  285.8 0.8 fusion.134
  286.6 3.1 copy-done
  289.8 3.1 fusion.22
  292.8 1.3 fusion.136
  294.1 10.0 %fusion.24 = f32[512,10,256]{0,2,1:T(8,128)} fusion(bf16[512,256,1]{1,0,2:T(8,128)(2,1)S(1)} %bitcast.166, f32[512,10,512]{0,2,1:T(8,128)} %copy-done, f32[512,10]{0,1:T(8,128)S(1)} %get-tuple-element.15, pred[512,512]{0,1:T(8,128)(4,1)S(1)} %copy-done.18), kind=kOutput, calls=%fused_computation.44 | convolution fusion | flops 1355284480 | bytes 16273408 | tf_op jit(solution)/shard_map/thk,kd->thd/dot_general | solution.py:39
  304.1 7.1 %fusion.20 = f32[512,10]{0,1:T(8,128)} fusion(f32[512,10,512]{0,2,1:T(8,128)} %get-tuple-element.53, f32[512,10]{0,1:T(8,128)S(1)} %get-tuple-element.16, pred[512,512]{0,1:T(8,128)(4,1)S(1)} %copy-done.17), kind=kLoop, calls=%fused_computation.40 | loop fusion | flops 13102080 | bytes 10788864 | tf_op jit(solution)/shard_map/reduce_sum | solution.py:38
  311.2 9.7 %fusion.26 = f32[512,10,256]{0,2,1:T(8,128)} fusion(bf16[512,256,1]{1,0,2:T(8,128)(2,1)S(1)} %bitcast.163, f32[512,10,512]{0,2,1:T(8,128)} %get-tuple-element.53, f32[512,10]{0,1:T(8,128)S(1)} %get-tuple-element.16, pred[512,512]{0,1:T(8,128)(4,1)S(1)} %copy-done.17), kind=kOutput, calls=%fused_computation.45 | convolution fusion | flops 1355284480 | bytes 16273408 | tf_op jit(solution)/shard_map/thk,kd->thd/dot_general | solution.py:39
  320.9 3.1 fusion.18
  324.0 10.0 %fusion.28 = f32[512,10,256]{0,2,1:T(8,128)} fusion(bf16[512,256,1]{1,0,2:T(8,128)(2,1)S(1)} %bitcast.161, f32[512,10,512]{0,2,1:T(8,128)} %get-tuple-element.55, f32[512,10]{0,1:T(8,128)S(1)} %get-tuple-element.17, pred[512,512]{0,1:T(8,128)(4,1)S(1)} %copy-done.16), kind=kOutput, calls=%fused_computation.46 | convolution fusion | flops 1355284480 | bytes 16273408 | tf_op jit(solution)/shard_map/thk,kd->thd/dot_general | solution.py:39
  334.1 3.1 fusion.16
  337.2 9.8 %fusion.30 = f32[512,10,256]{0,2,1:T(8,128)} fusion(bf16[512,256,1]{1,0,2:T(8,128)(2,1)S(1)} %bitcast.159, f32[512,10,512]{0,2,1:T(8,128)} %get-tuple-element.57, f32[512,10]{0,1:T(8,128)S(1)} %get-tuple-element.18, pred[512,512]{0,1:T(8,128)(4,1)S(1)} %copy-done.15), kind=kOutput, calls=%fused_computation.47 | convolution fusion | flops 1355284480 | bytes 16273408 | tf_op jit(solution)/shard_map/thk,kd->thd/dot_general | solution.py:39
  347.1 3.1 fusion.8
  350.2 3.1 fusion.14
  353.3 7.6 %fusion.12 = f32[512,10]{0,1:T(8,128)} fusion(f32[512,10,512]{0,2,1:T(8,128)} %get-tuple-element.61, f32[512,10]{0,1:T(8,128)} %get-tuple-element.20, pred[512,512]{0,1:T(8,128)(4,1)} %get-tuple-element.30), kind=kLoop, calls=%fused_computation.32 | loop fusion | flops 13102080 | bytes 10788864 | tf_op jit(solution)/shard_map/reduce_sum | solution.py:38
  361.0 3.1 fusion.10
  364.1 1.7 multiply_add_fusion
  365.8 5.6 %fusion.32 = f32[512,10,256]{0,2,1:T(8,128)} fusion(f32[512,10,512]{0,2,1:T(8,128)S(1)} %bitcast.145, f32[512,10]{0,1:T(8,128)} %copy-done.20, pred[512,512]{0,1:T(8,128)(4,1)} %copy-done.12, bf16[1,2048,256]{1,2,0:T(8,128)(2,1)S(1)} %copy-done.7), kind=kOutput, calls=%fused_computation.48 | convolution fusion | flops 1355284480 | bytes 16273408 | tf_op jit(solution)/shard_map/thk,kd->thd/dot_general | solution.py:39
  371.5 9.5 %fusion.34 = f32[512,10,256]{0,2,1:T(8,128)} fusion(f32[512,10,512]{0,2,1:T(8,128)} %get-tuple-element.61, f32[512,10]{0,1:T(8,128)S(1)} %copy-done.19, pred[512,512]{0,1:T(8,128)(4,1)S(1)} %copy-done.11, bf16[1,2048,256]{1,2,0:T(8,128)(2,1)S(1)} %copy-done.7), kind=kOutput, calls=%fused_computation.49 | convolution fusion | flops 1355284480 | bytes 16285696 | tf_op jit(solution)/shard_map/thk,kd->thd/dot_general | solution.py:39
  381.0 4.7 %fusion.36 = f32[512,10,256]{0,2,1:T(8,128)} fusion(f32[512,10,512]{0,2,1:T(8,128)S(1)} %bitcast.147, f32[512,10]{0,1:T(8,128)S(1)} %get-tuple-element.21, pred[512,512]{0,1:T(8,128)(4,1)S(1)} %copy-done.10, bf16[1,2048,256]{1,2,0:T(8,128)(2,1)S(1)} %copy-done.7), kind=kOutput, calls=%fused_computation.50 | convolution fusion | flops 1355284480 | bytes 16285696 | tf_op jit(solution)/shard_map/thk,kd->thd/dot_general | solution.py:39
  385.7 19.2 %divide_convert_fusion = bf16[512,10,256]{0,2,1:T(8,128)(2,1)} fusion(f32[512,10,256]{0,2,1:T(8,128)} %fusion.24, f32[512,10,256]{0,2,1:T(8,128)} %fusion.26, f32[512,10,256]{0,2,1:T(8,128)} %fusion.28, f32[512,10,256]{0,2,1:T(8,128)} %fusion.30, f32[512,10,256]{0,2,1:T(8,128)} %fusion.32, f32[512,10,256]{0,2,1:T(8,128)} %fusion.34, ...), kind=kOutput, calls=%fused_computation.52 | convolution fusion | flops 1377566720 | bytes 50536448 | tf_op jit(solution)/shard_map/thk,kd->thd/dot_general | solution.py:39
  404.9 12.0 %fusion.80 = bf16[1,512,2560]{2,1,0:T(8,128)(2,1)} fusion(bf16[512,2560]{0,1:T(8,128)(2,1)} %bitcast.168, bf16[2560,2560]{1,0:T(8,128)(2,1)} %param.13), kind=kOutput, calls=%fused_computation.96 | convolution fusion | flops 6712197120 | bytes 18350080 | tf_op jit(solution)/shard_map/dot_general | solution.py:131
  (137 shorter events, 3.2 us)
Async XLA Ops:
  7.2 37.2 %all-gather.8.cloned.1.call-start = ((), (), s32[]{:S(2)}) async-start(), calls=%async_computation.2 | async-start | bytes 1310720 | tf_op jit(solution)/shard_map/all_gather | solution.py:86
  17.2 37.9 %all-gather.18.cloned.1.call-start = ((), (), s32[]{:S(2)}) async-start(), calls=%async_computation.7 | async-start | bytes 1310720 | tf_op jit(solution)/shard_map/all_gather | solution.py:87
  19.1 125.2 %all-gather.10.cloned.1.call-start = ((), (), s32[]{:S(2)}) async-start(), calls=%async_computation.3 | async-start | bytes 5898240 | tf_op jit(solution)/shard_map/all_gather | solution.py:102
  19.8 210.9 %all-gather.14.cloned.1.call-start = ((), (), s32[]{:S(2)}) async-start(), calls=%async_computation.5 | async-start | bytes 5898240 | tf_op jit(solution)/shard_map/all_gather | solution.py:103
  20.4 12.2 %copy-start.30 = (s32[8,32]{1,0:T(8,128)S(1)}, s32[8,32]{1,0:T(8,128)}, u32[]{:S(2)}) copy-start(s32[8,32]{1,0:T(8,128)} %param.15) | copy-start | bytes 3076
  39.8 202.4 %copy-start.5 = (bf16[512,10,256]{2,0,1:T(8,128)(2,1)}, bf16[512,10,256]{2,0,1:T(8,128)(2,1)S(1)}, u32[]{:S(2)}) copy-start(bf16[512,10,256]{2,0,1:T(8,128)(2,1)S(1)} %pad_maximum_fusion) | copy-start | bytes 7864324
  43.2 23.5 %copy-start.12 = (pred[512,512]{0,1:T(8,128)(4,1)}, pred[512,512]{0,1:T(8,128)(4,1)S(1)}, u32[]{:S(2)}) copy-start(pred[512,512]{0,1:T(8,128)(4,1)S(1)} %get-tuple-element.29) | copy-start | bytes 786436
  46.4 203.0 %all-to-all-start = ((bf16[8,2,32,256]{3,2,1,0:T(8,128)(2,1)}), bf16[8,2,32,256]{3,2,1,0:T(8,128)(2,1)S(1)}, u32[]{:S(2)}, u32[]{:S(2)}) async-start(bf16[8,2,32,256]{3,2,1,0:T(8,128)(2,1)} %copy.86), calls=%async_computation | async-start | bytes 524288 | tf_op jit(solution)/shard_map/all_to_all | solution.py:164
  53.6 209.6 %all-gather.12.cloned.1.call-start = ((), (), s32[]{:S(2)}) async-start(), calls=%async_computation.4 | async-start | bytes 1310720 | tf_op jit(solution)/shard_map/all_gather | solution.py:111
  234.7 7.5 %copy-start.9 = (pred[512,512]{0,1:T(8,128)(4,1)S(1)}, pred[512,512]{0,1:T(8,128)(4,1)}, u32[]{:S(2)}) copy-start(pred[512,512]{0,1:T(8,128)(4,1)} %get-tuple-element.31) | copy-start | bytes 786436
  249.4 11.1 %copy-start.3 = (bf16[40,32,256]{2,1,0:T(8,128)(2,1)S(1)}, bf16[40,32,256]{2,1,0:T(8,128)(2,1)}, u32[]{:S(2)}) copy-start(bf16[40,32,256]{2,1,0:T(8,128)(2,1)} %copy.115) | copy-start | bytes 1966084
  249.4 12.2 %copy-start.1 = (bf16[40,32,256]{2,1,0:T(8,128)(2,1)S(1)}, bf16[40,32,256]{2,1,0:T(8,128)(2,1)}, u32[]{:S(2)}) copy-start(bf16[40,32,256]{2,1,0:T(8,128)(2,1)} %copy.116) | copy-start | bytes 1966084
  249.4 15.3 %copy-start.14 = (pred[512,512]{0,1:T(8,128)(4,1)S(1)}, pred[512,512]{0,1:T(8,128)(4,1)}, u32[]{:S(2)}) copy-start(pred[512,512]{0,1:T(8,128)(4,1)} %get-tuple-element.32) | copy-start | bytes 786436
  249.4 12.2 %all-to-all-start.1 = ((bf16[8,2,32,256]{3,2,1,0:T(8,128)(2,1)}), bf16[8,2,32,256]{3,2,1,0:T(8,128)(2,1)S(1)}, u32[]{:S(2)}, u32[]{:S(2)}) async-start(bf16[8,2,32,256]{3,2,1,0:T(8,128)(2,1)} %copy.89), calls=%async_computation.1 | async-start | bytes 524288 | tf_op jit(solution)/shard_map/all_to_all | solution.py:165
  253.0 39.8 %all-gather.16.cloned.1.call-start = ((), (), s32[]{:S(2)}) async-start(), calls=%async_computation.6 | async-start | bytes 1310720 | tf_op jit(solution)/shard_map/all_gather | solution.py:112
  260.5 25.3 %copy-start.26 = (f32[512,10]{0,1:T(8,128)}, f32[512,10]{0,1:T(8,128)S(1)}, u32[]{:S(2)}) copy-start(f32[512,10]{0,1:T(8,128)S(1)} %get-tuple-element.64) | copy-start | bytes 61444
  260.5 11.7 %copy-start.16 = (pred[512,512]{0,1:T(8,128)(4,1)S(1)}, pred[512,512]{0,1:T(8,128)(4,1)}, u32[]{:S(2)}) copy-start(pred[512,512]{0,1:T(8,128)(4,1)} %get-tuple-element.35) | copy-start | bytes 786436
  261.6 16.5 %copy-start.4 = (bf16[40,32,256]{2,1,0:T(8,128)(2,1)}, bf16[40,32,256]{2,1,0:T(8,128)(2,1)S(1)}, u32[]{:S(2)}) copy-start(bf16[40,32,256]{2,1,0:T(8,128)(2,1)S(1)} %scatter_fusion) | copy-start | bytes 1966084
  263.2 14.9 %copy-start.2 = (bf16[40,32,256]{2,1,0:T(8,128)(2,1)}, bf16[40,32,256]{2,1,0:T(8,128)(2,1)S(1)}, u32[]{:S(2)}) copy-start(bf16[40,32,256]{2,1,0:T(8,128)(2,1)S(1)} %scatter_fusion.1) | copy-start | bytes 1966084
  263.2 9.0 %copy-start.6 = (bf16[512,10,256]{2,0,1:T(8,128)(2,1)S(1)}, bf16[512,10,256]{2,0,1:T(8,128)(2,1)}, u32[]{:S(2)}) copy-start(bf16[512,10,256]{2,0,1:T(8,128)(2,1)} %copy-done.5) | copy-start | bytes 7864324
  272.3 5.8 %copy-start.17 = (pred[512,512]{0,1:T(8,128)(4,1)S(1)}, pred[512,512]{0,1:T(8,128)(4,1)}, u32[]{:S(2)}) copy-start(pred[512,512]{0,1:T(8,128)(4,1)} %get-tuple-element.34) | copy-start | bytes 786436
  278.0 5.8 %copy-start.18 = (pred[512,512]{0,1:T(8,128)(4,1)S(1)}, pred[512,512]{0,1:T(8,128)(4,1)}, u32[]{:S(2)}) copy-start(pred[512,512]{0,1:T(8,128)(4,1)} %get-tuple-element.33) | copy-start | bytes 786436
  283.9 1.9 copy-start.27
  283.9 1.9 copy-start.28
  283.9 1.9 copy-start.29
  285.8 4.0 copy-start
  286.6 17.5 %copy-start.21 = (f32[512,10]{0,1:T(8,128)}, f32[512,10]{0,1:T(8,128)S(1)}, u32[]{:S(2)}) copy-start(f32[512,10]{0,1:T(8,128)S(1)} %get-tuple-element.15) | copy-start | bytes 61444
  286.6 24.6 %copy-start.22 = (f32[512,10]{0,1:T(8,128)}, f32[512,10]{0,1:T(8,128)S(1)}, u32[]{:S(2)}) copy-start(f32[512,10]{0,1:T(8,128)S(1)} %get-tuple-element.16) | copy-start | bytes 61444
  286.6 37.5 %copy-start.23 = (f32[512,10]{0,1:T(8,128)}, f32[512,10]{0,1:T(8,128)S(1)}, u32[]{:S(2)}) copy-start(f32[512,10]{0,1:T(8,128)S(1)} %get-tuple-element.17) | copy-start | bytes 61444
  286.6 50.6 %copy-start.24 = (f32[512,10]{0,1:T(8,128)}, f32[512,10]{0,1:T(8,128)S(1)}, u32[]{:S(2)}) copy-start(f32[512,10]{0,1:T(8,128)S(1)} %get-tuple-element.18) | copy-start | bytes 61444
  286.6 60.5 %copy-start.25 = (f32[512,10]{0,1:T(8,128)}, f32[512,10]{0,1:T(8,128)S(1)}, u32[]{:S(2)}) copy-start(f32[512,10]{0,1:T(8,128)S(1)} %get-tuple-element.43) | copy-start | bytes 61444
  286.6 63.6 %copy-start.20 = (f32[512,10]{0,1:T(8,128)}, f32[512,10]{0,1:T(8,128)S(1)}, u32[]{:S(2)}) copy-start(f32[512,10]{0,1:T(8,128)S(1)} %get-tuple-element.19) | copy-start | bytes 61444
  294.1 26.8 %slice-start.12 = ((s8[10485760]{0:T(1024)(128)(4,1)}), s8[4194304]{0:T(1024)(128)(4,1)S(1)}, s32[]{:S(2)}) async-start(s8[10485760]{0:T(1024)(128)(4,1)} %bitcast.152), calls=%async_computation.20 | async-start | bytes 8388608
  294.1 26.8 %slice-start.13 = ((s8[10485760]{0:T(1024)(128)(4,1)}), s8[4194304]{0:T(1024)(128)(4,1)S(1)}, s32[]{:S(2)}) async-start(s8[10485760]{0:T(1024)(128)(4,1)} %bitcast.152), calls=%async_computation.21 | async-start | bytes 8388608
  311.2 9.8 %slice-start.14 = ((s8[10485760]{0:T(1024)(128)(4,1)}), s8[2097152]{0:T(1024)(128)(4,1)S(1)}, s32[]{:S(2)}) async-start(s8[10485760]{0:T(1024)(128)(4,1)} %bitcast.152), calls=%async_computation.22 | async-start | bytes 4194304
  311.2 22.9 %slice-start.9 = ((s8[10485760]{0:T(1024)(128)(4,1)}), s8[4194304]{0:T(1024)(128)(4,1)S(1)}, s32[]{:S(2)}) async-start(s8[10485760]{0:T(1024)(128)(4,1)} %bitcast.150), calls=%async_computation.17 | async-start | bytes 8388608
  311.2 22.9 %slice-start.10 = ((s8[10485760]{0:T(1024)(128)(4,1)}), s8[4194304]{0:T(1024)(128)(4,1)S(1)}, s32[]{:S(2)}) async-start(s8[10485760]{0:T(1024)(128)(4,1)} %bitcast.150), calls=%async_computation.18 | async-start | bytes 8388608
  324.0 10.1 %slice-start.11 = ((s8[10485760]{0:T(1024)(128)(4,1)}), s8[2097152]{0:T(1024)(128)(4,1)S(1)}, s32[]{:S(2)}) async-start(s8[10485760]{0:T(1024)(128)(4,1)} %bitcast.150), calls=%async_computation.19 | async-start | bytes 4194304
  324.0 23.0 %slice-start.6 = ((s8[10485760]{0:T(1024)(128)(4,1)}), s8[4194304]{0:T(1024)(128)(4,1)S(1)}, s32[]{:S(2)}) async-start(s8[10485760]{0:T(1024)(128)(4,1)} %bitcast.148), calls=%async_computation.14 | async-start | bytes 8388608
  324.0 23.0 %slice-start.7 = ((s8[10485760]{0:T(1024)(128)(4,1)}), s8[4194304]{0:T(1024)(128)(4,1)S(1)}, s32[]{:S(2)}) async-start(s8[10485760]{0:T(1024)(128)(4,1)} %bitcast.148), calls=%async_computation.15 | async-start | bytes 8388608
  334.1 3.1 copy-start.15
  337.2 13.0 %slice-start = ((s8[10485760]{0:T(1024)(128)(4,1)}), s8[4194304]{0:T(1024)(128)(4,1)S(1)}, s32[]{:S(2)}) async-start(s8[10485760]{0:T(1024)(128)(4,1)} %bitcast.144), calls=%async_computation.8 | async-start | bytes 8388608
  337.2 9.8 %slice-start.8 = ((s8[10485760]{0:T(1024)(128)(4,1)}), s8[2097152]{0:T(1024)(128)(4,1)S(1)}, s32[]{:S(2)}) async-start(s8[10485760]{0:T(1024)(128)(4,1)} %bitcast.148), calls=%async_computation.16 | async-start | bytes 4194304
  337.2 9.9 %copy-start.8 = (pred[512,512]{0,1:T(8,128)(4,1)S(1)}, pred[512,512]{0,1:T(8,128)(4,1)}, u32[]{:S(2)}) copy-start(pred[512,512]{0,1:T(8,128)(4,1)} %get-tuple-element.28) | copy-start | bytes 786436
  337.2 13.0 %slice-start.1 = ((s8[10485760]{0:T(1024)(128)(4,1)}), s8[4194304]{0:T(1024)(128)(4,1)S(1)}, s32[]{:S(2)}) async-start(s8[10485760]{0:T(1024)(128)(4,1)} %bitcast.144), calls=%async_computation.9 | async-start | bytes 8388608
  337.2 12.9 %slice-start.2 = ((s8[10485760]{0:T(1024)(128)(4,1)}), s8[2097152]{0:T(1024)(128)(4,1)S(1)}, s32[]{:S(2)}) async-start(s8[10485760]{0:T(1024)(128)(4,1)} %bitcast.144), calls=%async_computation.10 | async-start | bytes 4194304
  347.0 3.1 copy-start.13
  350.2 10.8 %slice-start.3 = ((s8[10485760]{0:T(1024)(128)(4,1)}), s8[4194304]{0:T(1024)(128)(4,1)S(1)}, s32[]{:S(2)}) async-start(s8[10485760]{0:T(1024)(128)(4,1)} %bitcast.146), calls=%async_computation.11 | async-start | bytes 8388608
  350.2 10.7 %slice-start.4 = ((s8[10485760]{0:T(1024)(128)(4,1)}), s8[4194304]{0:T(1024)(128)(4,1)S(1)}, s32[]{:S(2)}) async-start(s8[10485760]{0:T(1024)(128)(4,1)} %bitcast.146), calls=%async_computation.12 | async-start | bytes 8388608
  350.2 10.7 %copy-start.10 = (pred[512,512]{0,1:T(8,128)(4,1)S(1)}, pred[512,512]{0,1:T(8,128)(4,1)}, u32[]{:S(2)}) copy-start(pred[512,512]{0,1:T(8,128)(4,1)} %get-tuple-element.31) | copy-start | bytes 786436
  353.3 7.6 %slice-start.5 = ((s8[10485760]{0:T(1024)(128)(4,1)}), s8[2097152]{0:T(1024)(128)(4,1)S(1)}, s32[]{:S(2)}) async-start(s8[10485760]{0:T(1024)(128)(4,1)} %bitcast.146), calls=%async_computation.13 | async-start | bytes 4194304
  353.3 12.5 %copy-start.7 = (bf16[1,2048,256]{1,2,0:T(8,128)(2,1)S(1)}, bf16[1,2048,256]{1,2,0:T(8,128)(2,1)}, u32[]{:S(2)}) copy-start(bf16[1,2048,256]{1,2,0:T(8,128)(2,1)} %all-gather.18.cloned.1.call-done) | copy-start | bytes 3145732
  365.8 5.7 %copy-start.11 = (pred[512,512]{0,1:T(8,128)(4,1)S(1)}, pred[512,512]{0,1:T(8,128)(4,1)}, u32[]{:S(2)}) copy-start(pred[512,512]{0,1:T(8,128)(4,1)} %get-tuple-element.30) | copy-start | bytes 786436
  365.8 5.7 %copy-start.19 = (f32[512,10]{0,1:T(8,128)S(1)}, f32[512,10]{0,1:T(8,128)}, u32[]{:S(2)}) copy-start(f32[512,10]{0,1:T(8,128)} %get-tuple-element.20) | copy-start | bytes 61444
Sparse Core Ops, SparseCore 0:
  17.3 19.4 all-gather.7
  38.3 16.7 all-gather.17
  57.9 86.2 all-gather.9
  146.2 84.4 all-gather.13
  234.8 14.9 all-gather.11
  263.3 17.9 all-gather.15
where the time goes:
time: 430 us; the launch traced here: 424 us
  waiting for transfers between devices  163 us (38%)
  matrix products  142 us (33%)
  other arithmetic  52.5 us (12%)
  local copies, waits for them, and re-layouts  39.6 us (9%)
  between operations  15.6 us (4%)
  starting transfers between devices  11.3 us (3%)
    all_gather x1, waiting for transfers between devices, body(): lax.all_gather(value_cache, 'blk', axis=0, tiled=True)  83.5 us
    dot_general x8, matrix products, attend_block(): jnp.einsum('thk,kd->thd', weights.astype(jnp.bfloat16), value_rows, prefe...  78.6 us
    all_gather x1, waiting for transfers between devices, body(): lax.all_gather(key_cache, 'blk', axis=0, tiled=True)  77.5 us
    dot_general x8, matrix products, attend_block(): jnp.einsum('thd,kd->thk', query_block, key_rows, preferred_element_type=j...  50.5 us
    reduce_sum x8, other arithmetic, attend_block(): new_sum = running_sum * factor + jnp.sum(weights, axis=2)  33.2 us
    unnamed x96, local copies, waits for them, and re-layouts  13.4 us
    dot_general x1, matrix products, body(): jnp.dot(attended, out_weight, preferred_element_type=jnp.float32)  12 us
  transfers between devices with their start and end apart: 8, of which 3 were waited for; matrix products, arithmetic and copies ran while one was open for 23% of the time, Pallas kernels for 0%

commit v1 on v0

v1 whole, which is shorter than its diff:
```python
import jax
import jax.numpy as jnp
from jax import lax
from jax.experimental import pallas as pl
from jax.experimental.pallas import tpu as pltpu
from jax.sharding import PartitionSpec as P

masked_score = -1e30
half = 256
vmem_limit = 36 * 1024 * 1024
any_spec = pl.BlockSpec(memory_space=pl.ANY)
smem_spec = pl.BlockSpec(memory_space=pltpu.SMEM)
vmem_spec = pl.BlockSpec(memory_space=pltpu.VMEM)


def params():
    return pltpu.CompilerParams(vmem_limit_bytes=vmem_limit)


def turn(values, cosine, sine):
    front = values[:, :128].astype(jnp.float32)
    turned = front * cosine + pltpu.roll(front, 64, 1) * sine
    return turned


def pick_old_kernel(slots_ref, key_ref, value_ref, out_ref, sem):
    requests, cap = slots_ref.shape
    for r in range(requests):
        for c in range(cap):
            page = slots_ref[r, c]
            pltpu.make_async_copy(key_ref.at[page], out_ref.at[r, c, 0], sem).start()
            pltpu.make_async_copy(value_ref.at[page], out_ref.at[r, c, 1], sem).start()
    pltpu.make_async_copy(out_ref, out_ref, sem).wait()


def pick_old(slots, key_cache, value_cache):
    requests, cap = slots.shape
    return pl.pallas_call(
        pick_old_kernel,
        out_shape=jax.ShapeDtypeStruct((requests, cap, 2) + key_cache.shape[1:], jnp.bfloat16),
        in_specs=[smem_spec, any_spec, any_spec],
        out_specs=any_spec,
        scratch_shapes=[pltpu.SemaphoreType.DMA],
        compiler_params=params(),
        name="pick_old",
    )(slots, key_cache, value_cache)


def fresh_kernel(keys_ref, values_ref, cos_ref, sin_ref, out_ref):
    keys = keys_ref[...]
    out_ref[0, :, :128] = turn(keys, cos_ref[...], sin_ref[...]).astype(jnp.bfloat16)
    out_ref[0, :, 128:] = keys[:, 128:]
    out_ref[1] = values_ref[...]


def make_fresh(keys, values, cosine, sine):
    return pl.pallas_call(
        fresh_kernel,
        out_shape=jax.ShapeDtypeStruct((2,) + keys.shape, jnp.bfloat16),
        in_specs=[vmem_spec] * 4,
        out_specs=vmem_spec,
        compiler_params=params(),
        name="fresh",
    )(keys, values, cosine, sine)


def pick_new_kernel(info_ref, slots_ref, own_ref, core_ref, far_ref, far_core_ref, out_ref, sem):
    owners, cap = slots_ref.shape
    group_index = info_ref[0]
    rows = out_ref.shape[3]
    page_len = rows * 4
    block_pages = own_ref.shape[1] // page_len
    for o in range(owners):
        for c in range(cap):
            page = slots_ref[o, c]
            source = (page // block_pages) ^ group_index
            start = pl.multiple_of((page % block_pages) * page_len + rows * group_index, 32)
            for number, ref in enumerate((own_ref, core_ref, far_ref, far_core_ref)):

                @pl.when(source == number)
                def _():
                    pltpu.make_async_copy(
                        ref.at[:, pl.ds(start, rows), :], out_ref.at[o, c], sem
                    ).start()

    pltpu.make_async_copy(out_ref, out_ref, sem).wait()


def pick_new(info, slots, sources, rows):
    owners, cap = slots.shape
    return pl.pallas_call(
        pick_new_kernel,
        out_shape=jax.ShapeDtypeStruct(
            (owners, cap, 2, rows, sources[0].shape[2]), jnp.bfloat16
        ),
        in_specs=[smem_spec, smem_spec] + [any_spec] * 4,
        out_specs=any_spec,
        scratch_shapes=[pltpu.SemaphoreType.DMA],
        compiler_params=params(),
        name="pick_new",
    )(info, slots, *sources)


def lane_sums(weights):
    total = weights[:, :128]
    for start in range(128, weights.shape[1], 128):
        total = total + weights[:, start : start + 128]
    return total


def score(query, keys):
    return lax.dot_general(query, keys, (((1,), (1,)), ((), ())), preferred_element_type=jnp.float32)


def fresh_mask():
    row = lax.broadcasted_iota(jnp.int32, (half, half), 0)
    column = lax.broadcasted_iota(jnp.int32, (half, half), 1)
    return column <= row


def old_mask(pair):
    row = lax.broadcasted_iota(jnp.int32, (half, 128), 0)
    column = lax.broadcasted_iota(jnp.int32, (half, 128), 1)
    return column + (column // 64) * 64 + 64 * pair > row


def fetch_old(block, rest, slots_ref, sources, lows, kv_ref, sem):
    first = 4 * block
    later = list(range(first + 4, 16))
    order = later + [first + 2, first + 3, first, first + 1]
    for place, page in enumerate(order):
        slot = slots_ref[page]
        for source, low in zip(sources, lows):
            row = pl.multiple_of(rest + 64 * place + 32 * low, 32)
            pltpu.make_async_copy(source.at[slot], kv_ref.at[:, pl.ds(row, 32), :], sem).start()


def first_kernel(
    info_ref, slots_ref, query_ref, cos_ref, sin_ref, own_ref, core_ref, far_ref, far_core_ref,
    old_own_ref, old_core_ref, roped_ref, acc_ref, max_ref, sum_ref, kv_ref, sem,
):
    group_index = info_ref[0]
    has_old = info_ref[1]
    heads = acc_ref.shape[0]
    sources = (own_ref, core_ref, far_ref, far_core_ref)

    def run(block, with_old):
        low = block % 2
        rest = 512 * (block + 1)
        total = rest + (64 * (16 - 4 * block) if with_old else 0)
        own = sources[0]
        pltpu.make_async_copy(own.at[:, pl.ds(256, 256), :], kv_ref.at[:, pl.ds(0, 256), :], sem).start()
        pltpu.make_async_copy(own.at[:, pl.ds(0, 256), :], kv_ref.at[:, pl.ds(256, 256), :], sem).start()
        for earlier in range(block):
            pltpu.make_async_copy(
                sources[earlier ^ block], kv_ref.at[:, pl.ds(512 * (earlier + 1), 512), :], sem
            ).start()
        if with_old:
            fetch_old(block, rest, slots_ref, (old_own_ref, old_core_ref), (low, 1 - low), kv_ref, sem)
        filled = kv_ref.at[:, pl.ds(0, total), :]
        pltpu.make_async_copy(filled, filled, sem).wait()
        lower = fresh_mask()
        upper = old_mask(block // 2)

        def head(h, carry):
            columns = pl.ds(pl.multiple_of(h * 256, 256), 256)
            for part in range(2):
                rows = pl.ds(part * half, half)
                raw = query_ref[rows, columns]
                front = turn(raw, cos_ref[rows, :], sin_ref[rows, :])
                query = jnp.concatenate(
                    [(front * 0.0625).astype(jnp.bfloat16), raw[:, 128:] * jnp.bfloat16(0.0625)], axis=1
                )
                roped_ref[h, rows, :] = query
                start = 256 if part == 0 else 0
                stop = total - 128 if with_old and part == 1 else total
                keys = kv_ref[0, pl.ds(start, stop - start), :]
                values = kv_ref[1, pl.ds(start, stop - start), :]
                scores = score(query, keys)
                pieces = [jnp.where(lower, scores[:, :256], masked_score)]
                if with_old:
                    pieces.append(scores[:, 256 : stop - start - 128])
                    pieces.append(jnp.where(upper, scores[:, stop - start - 128 :], masked_score))
                elif stop - start > 256:
                    pieces.append(scores[:, 256:])
                scores = jnp.concatenate(pieces, axis=1) if len(pieces) > 1 else pieces[0]
                top = jnp.max(scores, axis=1, keepdims=True)
                weights = jnp.exp(scores - top)
                acc_ref[h, rows, :] = jnp.dot(
                    weights.astype(jnp.bfloat16), values, preferred_element_type=jnp.float32
                )
                max_ref[h, rows, :] = jnp.broadcast_to(top, (half, 128))
                sum_ref[h, rows, :] = lane_sums(weights)
            return carry

        lax.fori_loop(0, heads, head, 0)

    for block in range(4):
        for with_old in (False, True):

            @pl.when((group_index == block) & (has_old == int(with_old)))
            def _(block=block, with_old=with_old):
                run(block, with_old)


def first_part(info, slots, queries, cosine, sine, sources, old_own, old_core):
    tokens, width = queries.shape
    heads = width // 256
    return pl.pallas_call(
        first_kernel,
        out_shape=(
            pltpu.VMEM((heads, tokens, 256), jnp.bfloat16),
            pltpu.VMEM((heads, tokens, 256), jnp.float32),
            pltpu.VMEM((heads, tokens, 128), jnp.float32),
            pltpu.VMEM((heads, tokens, 128), jnp.float32),
        ),
        in_specs=[smem_spec, smem_spec, vmem_spec, vmem_spec, vmem_spec] + [any_spec] * 6,
        out_specs=(vmem_spec,) * 4,
        scratch_shapes=[pltpu.VMEM((2, 2304, 256), jnp.bfloat16), pltpu.SemaphoreType.DMA],
        compiler_params=params(),
        name="attend_first",
    )(info, slots, queries, cosine, sine, *sources, old_own, old_core)


def second_kernel(
    info_ref, slots_ref, pool_ref, roped_ref, acc_ref, max_ref, sum_ref, far_ref, far_core_ref,
    weight_ref, arrived_ref, key_ref, value_ref, hidden_ref, key_out_ref, value_out_ref,
    kv_ref, attended_ref, w_ref, stage_ref, sem, weight_sems, pool_sem, out_sems,
):
    group_index = info_ref[0]
    has_old = info_ref[1]
    heads = acc_ref.shape[0]
    chunks = weight_ref.shape[1] // 512

    def weight_copy(n):
        return pltpu.make_async_copy(
            weight_ref.at[:, pl.ds(n * 512, 512)], w_ref.at[n], weight_sems.at[n]
        )

    def run(block):
        fetch_old(
            block, 0, slots_ref, (far_ref, far_core_ref), (block % 2, 1 - block % 2), kv_ref, sem
        )

    def attend(block):
        total = 64 * (16 - 4 * block)
        filled = kv_ref.at[:, pl.ds(0, total), :]
        pltpu.make_async_copy(filled, filled, sem).wait()
        upper = old_mask(1 - block // 2)

        def head(h, carry):
            columns = pl.ds(pl.multiple_of(h * 256, 256), 256)
            for part in range(2):
                rows = pl.ds(part * half, half)
                stop = total - 128 * part
                scores = score(roped_ref[h, rows, :], kv_ref[0, pl.ds(0, stop), :])
                last = jnp.where(upper, scores[:, stop - 128 :], masked_score)
                scores = (
                    jnp.concatenate([scores[:, : stop - 128], last], axis=1) if stop > 128 else last
                )
                before = max_ref[h, rows, :][:, :1]
                top = jnp.maximum(before, jnp.max(scores, axis=1, keepdims=True))
                factor = jnp.exp(before - top)
                weights = jnp.exp(scores - top)
                total_sum = jnp.sum(sum_ref[h, rows, :] * factor + lane_sums(weights), axis=1, keepdims=True)
                mixed = acc_ref[h, rows, :] * factor + jnp.dot(
                    weights.astype(jnp.bfloat16), kv_ref[1, pl.ds(0, stop), :],
                    preferred_element_type=jnp.float32,
                )
                attended_ref[rows, columns] = (mixed / total_sum).astype(jnp.bfloat16)
            return carry

        lax.fori_loop(0, heads, head, 0)

    for block in range(4):

        @pl.when((group_index == block) & (has_old == 1))
        def _(block=block):
            run(block)

    for n in range(chunks):
        weight_copy(n).start()

    def place(page, carry):
        slot = pool_ref[page]

        @pl.when(slot >= 0)
        def _():
            pltpu.make_async_copy(arrived_ref.at[slot, 0], key_out_ref.at[page], pool_sem).start()
            pltpu.make_async_copy(arrived_ref.at[slot, 1], value_out_ref.at[page], pool_sem).start()

        @pl.when(slot < 0)
        def _():
            pltpu.make_async_copy(key_ref.at[page], key_out_ref.at[page], pool_sem).start()
            pltpu.make_async_copy(value_ref.at[page], value_out_ref.at[page], pool_sem).start()

        return carry

    lax.fori_loop(0, key_ref.shape[0], place, 0)

    for block in range(4):

        @pl.when((group_index == block) & (has_old == 1))
        def _(block=block):
            attend(block)

    @pl.when(has_old == 0)
    def _():
        def head(h, carry):
            columns = pl.ds(pl.multiple_of(h * 256, 256), 256)
            total_sum = jnp.sum(sum_ref[h], axis=1, keepdims=True)
            attended_ref[:, columns] = (acc_ref[h] / total_sum).astype(jnp.bfloat16)
            return carry

        lax.fori_loop(0, heads, head, 0)

    for n in range(chunks):
        weight_copy(n).wait()
        stage_ref[n] = jnp.dot(
            attended_ref[...], w_ref[n], preferred_element_type=jnp.float32
        ).astype(jnp.bfloat16)
        pltpu.make_async_copy(stage_ref.at[n], hidden_ref.at[:, pl.ds(n * 512, 512)], out_sems.at[n]).start()
    for n in range(chunks):
        pltpu.make_async_copy(stage_ref.at[n], hidden_ref.at[:, pl.ds(n * 512, 512)], out_sems.at[n]).wait()
    pltpu.make_async_copy(key_out_ref, key_out_ref, pool_sem).wait()
    pltpu.make_async_copy(value_out_ref, value_out_ref, pool_sem).wait()


def second_part(info, slots, pool, state, far, far_core, weight, arrived, key_cache, value_cache):
    heads, tokens, _ = state[0].shape
    width = weight.shape[1]
    chunks = width // 512
    state = [pltpu.with_memory_space_constraint(part, pltpu.VMEM) for part in state]
    return pl.pallas_call(
        second_kernel,
        out_shape=(
            jax.ShapeDtypeStruct((tokens, width), jnp.bfloat16),
            jax.ShapeDtypeStruct(key_cache.shape, jnp.bfloat16),
            jax.ShapeDtypeStruct(value_cache.shape, jnp.bfloat16),
        ),
        in_specs=[smem_spec] * 3 + [vmem_spec] * 4 + [any_spec] * 6,
        out_specs=(any_spec,) * 3,
        scratch_shapes=[
            pltpu.VMEM((2, 1024, 256), jnp.bfloat16),
            pltpu.VMEM((tokens, weight.shape[0]), jnp.bfloat16),
            pltpu.VMEM((chunks, weight.shape[0], 512), jnp.bfloat16),
            pltpu.VMEM((chunks, tokens, 512), jnp.bfloat16),
            pltpu.SemaphoreType.DMA,
            pltpu.SemaphoreType.DMA((chunks,)),
            pltpu.SemaphoreType.DMA,
            pltpu.SemaphoreType.DMA((chunks,)),
        ],
        compiler_params=params(),
        name="attend_second",
    )(info, slots, pool, *state, far, far_core, weight, arrived, key_cache, value_cache)


def body(queries, new_keys, new_values, key_cache, value_cache, out_weight, lengths, page_table):
    blk_count = lax.axis_size("blk")
    blk_index = lax.axis_index("blk")
    group_count = lax.axis_size("group")
    group_index = lax.axis_index("group")
    tok_rows = queries.shape[1]
    pages_here, page_rows, head_dim = key_cache.shape
    slot_count = page_table.shape[1]
    fresh_pages = tok_rows * group_count // (page_rows * group_count)
    window_pages = slot_count - fresh_pages
    cap_old = (window_pages + blk_count - 1) // blk_count
    cap_new = (fresh_pages + blk_count - 1) // blk_count

    owner = page_table // pages_here
    local = page_table % pages_here
    columns = jnp.arange(slot_count, dtype=jnp.int32)
    same_kind = (columns[:, None] >= window_pages) == (columns[None, :] >= window_pages)
    earlier = same_kind & (columns[None, :] < columns[:, None])
    rank = jnp.sum(
        (earlier[None] & (owner[:, None, :] == owner[:, :, None])).astype(jnp.int32), axis=2
    )
    here = owner == blk_index
    ranks_old = jnp.arange(cap_old, dtype=jnp.int32)
    old_send = jnp.sum(
        jnp.where(
            here[:, None, :window_pages] & (rank[:, None, :window_pages] == ranks_old[None, :, None]),
            local[:, None, :window_pages],
            0,
        ),
        axis=2,
    )
    my_owner = owner[blk_index]
    my_rank = rank[blk_index]
    old_slots = my_owner[:window_pages] * cap_old + my_rank[:window_pages]
    new_slots = my_owner[window_pages:] * cap_new + my_rank[window_pages:]
    new_send = jnp.sum(
        jnp.where(
            new_slots[None, :] == jnp.arange(blk_count * cap_new, dtype=jnp.int32)[:, None],
            jnp.arange(fresh_pages, dtype=jnp.int32)[None, :],
            0,
        ),
        axis=1,
    ).reshape(blk_count, cap_new)
    sent_as = jnp.arange(blk_count, dtype=jnp.int32)[:, None] * cap_new + rank[:, window_pages:]
    lands = here[:, window_pages:].reshape(1, -1) & (
        local[:, window_pages:].reshape(1, -1) == jnp.arange(pages_here, dtype=jnp.int32)[:, None]
    )
    pool = jnp.max(jnp.where(lands, sent_as.reshape(1, -1), -1), axis=1)
    length = lengths[blk_index]
    info = jnp.stack([group_index, (length > 0).astype(jnp.int32)])

    old_out = pick_old(old_send, key_cache, value_cache)
    old_own = lax.all_to_all(old_out, "blk", split_axis=0, concat_axis=0, tiled=True)
    old_own = old_own.reshape((blk_count * cap_old,) + old_own.shape[2:])

    positions = length + group_index * tok_rows + jnp.arange(tok_rows, dtype=jnp.int32)
    quarter = head_dim // 4
    freq_table = 10000.0 ** (-jnp.arange(quarter, dtype=jnp.float32) / quarter)
    angles = positions.astype(jnp.float32)[:, None] * freq_table
    cosine = jnp.cos(angles)
    sine = jnp.sin(angles)
    cosine = jnp.concatenate([cosine, cosine], axis=1)
    sine = jnp.concatenate([-sine, sine], axis=1)
    fresh = make_fresh(new_keys[0], new_values[0], cosine, sine)

    swap_core = [(0, 1), (1, 0), (2, 3), (3, 2)]
    swap_chip = [(0, 2), (2, 0), (1, 3), (3, 1)]
    far = lax.ppermute(fresh, "group", swap_chip)
    core = lax.ppermute(fresh, "group", swap_core)
    far_core = lax.ppermute(far, "group", swap_core)
    sources = (fresh, core, far, far_core)

    old_far = lax.ppermute(old_own, "group", swap_chip)
    old_core = lax.ppermute(old_own, "group", swap_core)
    old_far_core = lax.ppermute(old_far, "group", swap_core)

    new_out = pick_new(info, new_send, sources, page_rows)
    arrived = lax.all_to_all(new_out, "blk", split_axis=0, concat_axis=0, tiled=True)
    arrived = arrived.reshape((blk_count * cap_new,) + arrived.shape[2:])

    state = first_part(
        info, old_slots, queries[0], cosine, sine, sources, old_own, old_core
    )
    hidden, key_out, value_out = second_part(
        info, old_slots, pool, state, old_far, old_far_core, out_weight, arrived, key_cache, value_cache
    )
    return (hidden[None], key_out, value_out)


def solution(mesh):
    return jax.shard_map(
        body,
        mesh=mesh,
        in_specs=(
            P("blk", "group", None),
            P("blk", "group", None),
            P("blk", "group", None),
            P("blk", "group", None),
            P("blk", "group", None),
            P(),
            P(),
            P(),
        ),
        out_specs=(P("blk", "group", None), P("blk", "group", None), P("blk", "group", None)),
        check_vma=False,
    )
```

time: 430 us -> 116 us (0.27)
  the two profiles are of different devices: /device:TPU:0 before, /device:TPU:7 now
where the time goes in v1:
time: 116 us; the launch traced here: 115 us
  Pallas kernels  54.5 us (47%)
  local copies, waits for them, and re-layouts  21.8 us (19%)
  starting transfers between devices  17.2 us (15%)
  waiting for transfers between devices  15.1 us (13%)
  other arithmetic  3.6 us (3%)
  between operations  2.34 us (2%)
    pallas_call x1, Pallas kernels, first_part(): pl.pallas_call(first_kernel, out_shape=(pltpu.VMEM((heads, tokens, 256),...  26.8 us
    pallas_call x1, Pallas kernels, second_part(): pl.pallas_call(second_kernel, out_shape=(jax.ShapeDtypeStruct((tokens, wi...  24.7 us
    unnamed x46, local copies, waits for them, and re-layouts  20.8 us
    ppermute x1, waiting for transfers between devices, body(): far = lax.ppermute(fresh, 'group', swap_chip)  10.4 us
    all_to_all x1, starting transfers between devices, body(): lax.all_to_all(old_out, 'blk', split_axis=0, concat_axis=0, tiled=True)  5.79 us
    all_to_all x1, starting transfers between devices, body(): lax.all_to_all(new_out, 'blk', split_axis=0, concat_axis=0, tiled=True)  5.45 us
    ppermute x1, waiting for transfers between devices, body(): old_far = lax.ppermute(old_own, 'group', swap_chip)  4.41 us
  transfers between devices with their start and end apart: 8, of which 3 were waited for; matrix products, arithmetic and copies ran while one was open for 2% of the time, Pallas kernels for 25%

profile of v1, /device:TPU:7, one launch (start us, length us, event | category | flops | bytes accessed | tf_op | source)
XLA Modules:
  0.0 114.6 jit_solution(4815339177702370922)
XLA Ops:
  0.6 0.0 copy-start.22
  0.7 0.1 fusion.2
  0.7 0.7 add_select_fusion
  1.4 0.7 broadcast_compare_fusion
  2.1 0.1 fusion.7
  2.2 0.3 convert_reduce_fusion
  2.5 0.1 fusion.5
  2.6 0.2 select_reduce_fusion.2
  2.7 0.1 copy.11.slots_ref
  2.8 1.1 copy-done.6
  3.9 1.1 copy-done.8
  5.0 1.4 %pick_old.1 = bf16[8,2,2,32,256]{4,3,2,1,0:T(8,128)(2,1)} custom-call(s32[8,2]{1,0:T(8,128)S(1)} %copy.11.slots_ref, bf16[40,32,256]{2,1,0:T(8,128)(2,1)S(1)} %copy-done.6, bf16[40,32,256]{2,1,0:T(8,128)(2,1)S(1)} %copy-done.8), custom_call_target="tpu_custom_call" | custom-call | tf_op jit(solution)/shard_map/pick_old/pallas_call | solution.py:38
  6.4 5.8 %all-to-all-start = ((bf16[8,2,2,32,256]{4,3,2,1,0:T(8,128)(2,1)}), bf16[8,2,2,32,256]{4,3,2,1,0:T(8,128)(2,1)S(1)}, u32[]{:S(2)}, u32[]{:S(2)}) async-start(bf16[8,2,2,32,256]{4,3,2,1,0:T(8,128)(2,1)} %pick_old.1), calls=%async_computation | async-start | bytes 1048576 | tf_op jit(solution)/shard_map/all_to_all | solution.py:410
  12.2 0.0 copy-done.22
  12.2 0.6 dynamic_slice.9
  13.5 1.0 fusion
  14.5 0.2 pad_maximum_fusion
  14.7 0.0 copy-start.10
  14.7 0.0 copy-done.20
  14.7 0.1 fresh.1.own_ref
  14.8 0.3 collective-permute-start.1
  15.1 1.5 %collective-permute-start = (bf16[2,512,256]{2,1,0:T(8,128)(2,1)S(1)}, bf16[2,512,256]{2,1,0:T(8,128)(2,1)S(1)}, u32[]{:S(2)}, u32[]{:S(2)}) collective-permute-start(bf16[2,512,256]{2,1,0:T(8,128)(2,1)S(1)} %fresh.1.own_ref), channel_id=1, source_target_pairs={{0,1},{1,0},{2,3},{3,2},{4,5},{5,4},{6,7},{7,6},{8,9},{9,8},{10,11... | collective-permute-start | bytes 1572872 | tf_op jit(solution)/shard_map/ppermute | solution.py:426
  16.6 10.4 %collective-permute-done.1.far_ref = bf16[2,512,256]{2,1,0:T(8,128)(2,1)S(1)} collective-permute-done((bf16[2,512,256]{2,1,0:T(8,128)(2,1)S(1)}, bf16[2,512,256]{2,1,0:T(8,128)(2,1)S(1)}, u32[]{:S(2)}, u32[]{:S(2)}) %collective-permute-start.1) | collective-permute-done | bytes 524320 | tf_op jit(solution)/shard_map/ppermute | solution.py:425
  27.1 2.2 %collective-permute-start.2 = (bf16[2,512,256]{2,1,0:T(8,128)(2,1)S(1)}, bf16[2,512,256]{2,1,0:T(8,128)(2,1)S(1)}, u32[]{:S(2)}, u32[]{:S(2)}) collective-permute-start(bf16[2,512,256]{2,1,0:T(8,128)(2,1)S(1)} %collective-permute-done.1.far_ref), channel_id=1, source_target_pairs={{0,1},{1,0},{2,3},{3,2},{4,5},{5,4},{6,7},{7,6},{8,9},{9,8},{10,11... | collective-permute-start | bytes 1572872 | tf_op jit(solution)/shard_map/ppermute | solution.py:427
  29.2 0.1 add_bitcast_fusion
  29.3 0.0 all-to-all-done
  29.3 0.3 collective-permute-start.4
  29.6 0.1 select_reduce_fusion.1
  30.3 0.1 reshape.100.slots_ref
  30.4 0.1 pad_add_fusion.info_ref
  30.5 0.0 collective-permute-done.core_ref
  30.5 0.3 collective-permute-done.2.far_core_ref
  30.8 1.4 %pick_new.1 = bf16[8,2,2,32,256]{4,3,2,1,0:T(8,128)(2,1)} custom-call(s32[2]{0:T(128)S(1)} %pad_add_fusion.info_ref, s32[8,2]{1,0:T(8,128)S(1)} %reshape.100.slots_ref, bf16[2,512,256]{2,1,0:T(8,128)(2,1)S(1)} %fresh.1.own_ref, bf16[2,512,256]{2,1,0:T(8,128)(2,1)S(1)} %collective-permute-done.core_ref, ...), custom_call_target="tpu_custom_call" | custom-call | tf_op jit(solution)/shard_map/pick_new/pallas_call | solution.py:91
  32.2 5.4 %all-to-all-start.1 = ((bf16[8,2,2,32,256]{4,3,2,1,0:T(8,128)(2,1)}), bf16[8,2,2,32,256]{4,3,2,1,0:T(8,128)(2,1)}, u32[]{:S(2)}, u32[]{:S(2)}) async-start(bf16[8,2,2,32,256]{4,3,2,1,0:T(8,128)(2,1)} %pick_new.1), calls=%async_computation.1 | async-start | bytes 1048576 | tf_op jit(solution)/shard_map/all_to_all | solution.py:435
  37.7 0.9 collective-permute-start.3
  38.6 4.4 %collective-permute-done.4.far_ref = bf16[16,2,32,256]{3,2,1,0:T(8,128)(2,1)} collective-permute-done((bf16[16,2,32,256]{3,2,1,0:T(8,128)(2,1)S(1)}, bf16[16,2,32,256]{3,2,1,0:T(8,128)(2,1)}, u32[]{:S(2)}, u32[]{:S(2)}) %collective-permute-start.4) | collective-permute-done | bytes 524320 | tf_op jit(solution)/shard_map/ppermute | solution.py:430
  43.0 0.8 collective-permute-start.5
  43.8 0.1 and.47
  43.9 0.1 broadcast_in_dim.40
  44.0 0.1 eq.89
  44.0 0.1 select_reduce_fusion.pool_ref
  44.2 0.0 collective-permute-done.3.old_core_ref
  44.2 0.0 copy-done.14
  44.2 0.0 copy-done.12
  44.2 0.0 copy-done.16
  44.2 0.0 copy-done.18
  44.2 0.0 copy-start.11
  44.2 0.9 copy-done.11
  45.2 1.0 copy-done.13
  46.2 1.0 copy-done.15
  47.3 1.0 copy-done.17
  48.3 1.0 copy-done.19
  49.3 26.8 %attend_first.1 = (bf16[10,512,256]{2,1,0:T(8,128)(2,1)S(1)}, f32[10,512,256]{2,1,0:T(8,128)S(1)}, f32[10,512,128]{2,1,0:T(8,128)S(1)}, f32[10,512,128]{2,1,0:T(8,128)S(1)}) custom-call(s32[2]{0:T(128)S(1)} %pad_add_fusion.info_ref, s32[16]{0:T(128)S(1)} %get-tuple-element.27.slots_ref, bf16[512,2560]{1,0:T(8,128)(2,1)} %bitcast.18, ...), custom_call_target="tpu_custom_call" | custom-call | tf_op jit(solution)/shard_map/attend_first/pallas_call | solution.py:209
  76.2 2.3 %copy-done = f32[10,512,256]{2,1,0:T(8,128)} copy-done((f32[10,512,256]{2,1,0:T(8,128)}, f32[10,512,256]{2,1,0:T(8,128)S(1)}, u32[]{:S(2)}) %copy-start) | copy-done | bytes 5242904
  78.5 1.5 %copy-done.2 = f32[10,512,128]{2,1,0:T(8,128)} copy-done((f32[10,512,128]{2,1,0:T(8,128)}, f32[10,512,128]{2,1,0:T(8,128)S(1)}, u32[]{:S(2)}) %copy-start.2) | copy-done | bytes 2621464
  80.0 1.5 %copy-done.4 = f32[10,512,128]{2,1,0:T(8,128)} copy-done((f32[10,512,128]{2,1,0:T(8,128)}, f32[10,512,128]{2,1,0:T(8,128)S(1)}, u32[]{:S(2)}) %copy-start.4) | copy-done | bytes 2621464
  81.5 0.0 collective-permute-done.5.far_core_ref
  81.5 0.0 all-to-all-done.1
  81.5 2.5 %copy-done.1 = f32[10,512,256]{2,1,0:T(8,128)S(1)} copy-done((f32[10,512,256]{2,1,0:T(8,128)S(1)}, f32[10,512,256]{2,1,0:T(8,128)}, u32[]{:S(2)}) %copy-start.1) | copy-done | bytes 5242904
  84.0 1.7 %copy-done.3 = f32[10,512,128]{2,1,0:T(8,128)S(1)} copy-done((f32[10,512,128]{2,1,0:T(8,128)S(1)}, f32[10,512,128]{2,1,0:T(8,128)}, u32[]{:S(2)}) %copy-start.3) | copy-done | bytes 2621464
  85.7 1.7 %copy-done.5 = f32[10,512,128]{2,1,0:T(8,128)S(1)} copy-done((f32[10,512,128]{2,1,0:T(8,128)S(1)}, f32[10,512,128]{2,1,0:T(8,128)}, u32[]{:S(2)}) %copy-start.5) | copy-done | bytes 2621464
  87.5 1.1 copy-done.7
  88.6 1.1 copy-done.9
  89.6 24.7 %attend_second.1 = (bf16[512,2560]{1,0:T(8,128)(2,1)}, bf16[40,32,256]{2,1,0:T(8,128)(2,1)}, bf16[40,32,256]{2,1,0:T(8,128)(2,1)}) custom-call(s32[2]{0:T(128)S(1)} %pad_add_fusion.info_ref, s32[16]{0:T(128)S(1)} %get-tuple-element.27.slots_ref, s32[40]{0:T(128)S(1)} %select_reduce_fusion.pool_ref, bf16[10,512,256]{2,1,0:T(8,128)(2,1)S(1)} %get-tuple-element.10.roped_ref, ...), custom_call_target="tpu_custom_call" | custom-call | tf_op jit(solution)/shard_map/attend_second/pallas_call | solution.py:334
  (27 shorter events, 0.1 us)
Async XLA Ops:
  0.6 11.6 %copy-start.22 = (s32[8]{0:T(128)S(1)}, s32[8]{0:T(128)}, u32[]{:S(2)}) copy-start(s32[8]{0:T(128)} %param.14) | copy-start | bytes 100
  2.8 1.1 copy-start.6
  3.9 1.1 copy-start.8
  5.0 9.7 %copy-start.20 = (bf16[1,512,256]{2,1,0:T(8,128)(2,1)S(1)}, bf16[1,512,256]{2,1,0:T(8,128)(2,1)}, u32[]{:S(2)}) copy-start(bf16[1,512,256]{2,1,0:T(8,128)(2,1)} %param.9) | copy-start | bytes 786436
  5.0 9.7 %copy-start.21 = (bf16[1,512,256]{2,1,0:T(8,128)(2,1)S(1)}, bf16[1,512,256]{2,1,0:T(8,128)(2,1)}, u32[]{:S(2)}) copy-start(bf16[1,512,256]{2,1,0:T(8,128)(2,1)} %param.10) | copy-start | bytes 786436
  6.4 22.9 %all-to-all-start = ((bf16[8,2,2,32,256]{4,3,2,1,0:T(8,128)(2,1)}), bf16[8,2,2,32,256]{4,3,2,1,0:T(8,128)(2,1)S(1)}, u32[]{:S(2)}, u32[]{:S(2)}) async-start(bf16[8,2,2,32,256]{4,3,2,1,0:T(8,128)(2,1)} %pick_old.1), calls=%async_computation | async-start | bytes 1048576 | tf_op jit(solution)/shard_map/all_to_all | solution.py:410
  14.7 17.5 %copy-start.10 = (f32[512,128]{1,0:T(8,128)}, f32[512,128]{1,0:T(8,128)S(1)}, u32[]{:S(2)}) copy-start(f32[512,128]{1,0:T(8,128)S(1)} %get-tuple-element.33.sin_ref) | copy-start | bytes 786436
  14.8 12.2 %collective-permute-start.1 = (bf16[2,512,256]{2,1,0:T(8,128)(2,1)S(1)}, bf16[2,512,256]{2,1,0:T(8,128)(2,1)S(1)}, u32[]{:S(2)}, u32[]{:S(2)}) collective-permute-start(bf16[2,512,256]{2,1,0:T(8,128)(2,1)S(1)} %fresh.1.own_ref), channel_id=1, source_target_pairs={{0,2},{2,0},{1,3},{3,1},{4,6},{6,4},{5,7},{7,5},{8,10},{10,8},{9,1... | collective-permute-start | bytes 1572872 | tf_op jit(solution)/shard_map/ppermute | solution.py:425
  15.1 15.4 %collective-permute-start = (bf16[2,512,256]{2,1,0:T(8,128)(2,1)S(1)}, bf16[2,512,256]{2,1,0:T(8,128)(2,1)S(1)}, u32[]{:S(2)}, u32[]{:S(2)}) collective-permute-start(bf16[2,512,256]{2,1,0:T(8,128)(2,1)S(1)} %fresh.1.own_ref), channel_id=1, source_target_pairs={{0,1},{1,0},{2,3},{3,2},{4,5},{5,4},{6,7},{7,6},{8,9},{9,8},{10,11... | collective-permute-start | bytes 1572872 | tf_op jit(solution)/shard_map/ppermute | solution.py:426
  27.1 17.1 %copy-start.14 = (bf16[2,512,256]{2,1,0:T(8,128)(2,1)}, bf16[2,512,256]{2,1,0:T(8,128)(2,1)S(1)}, u32[]{:S(2)}) copy-start(bf16[2,512,256]{2,1,0:T(8,128)(2,1)S(1)} %collective-permute-done.1.far_ref) | copy-start | bytes 1572868
  27.1 3.7 %collective-permute-start.2 = (bf16[2,512,256]{2,1,0:T(8,128)(2,1)S(1)}, bf16[2,512,256]{2,1,0:T(8,128)(2,1)S(1)}, u32[]{:S(2)}, u32[]{:S(2)}) collective-permute-start(bf16[2,512,256]{2,1,0:T(8,128)(2,1)S(1)} %collective-permute-done.1.far_ref), channel_id=1, source_target_pairs={{0,1},{1,0},{2,3},{3,2},{4,5},{5,4},{6,7},{7,6},{8,9},{9,8},{10,11... | collective-permute-start | bytes 1572872 | tf_op jit(solution)/shard_map/ppermute | solution.py:427
  29.3 14.9 %copy-start.12 = (bf16[8,2,2,32,256]{4,3,2,1,0:T(8,128)(2,1)}, bf16[8,2,2,32,256]{4,3,2,1,0:T(8,128)(2,1)S(1)}, u32[]{:S(2)}) copy-start(bf16[8,2,2,32,256]{4,3,2,1,0:T(8,128)(2,1)S(1)} %all-to-all-done) | copy-start | bytes 1572868
  29.3 13.7 %collective-permute-start.4 = (bf16[16,2,32,256]{3,2,1,0:T(8,128)(2,1)S(1)}, bf16[16,2,32,256]{3,2,1,0:T(8,128)(2,1)}, u32[]{:S(2)}, u32[]{:S(2)}) collective-permute-start(bf16[16,2,32,256]{3,2,1,0:T(8,128)(2,1)S(1)} %bitcast.13), channel_id=1, source_target_pairs={{0,2},{2,0},{1,3},{3,1},{4,6},{6,4},{5,7},{7,5},{8,10},{10,8},{9,1... | collective-permute-start | bytes 1572872 | tf_op jit(solution)/shard_map/ppermute | solution.py:430
  30.5 13.7 %copy-start.16 = (bf16[2,512,256]{2,1,0:T(8,128)(2,1)}, bf16[2,512,256]{2,1,0:T(8,128)(2,1)S(1)}, u32[]{:S(2)}) copy-start(bf16[2,512,256]{2,1,0:T(8,128)(2,1)S(1)} %collective-permute-done.core_ref) | copy-start | bytes 1572868
  30.8 13.4 %copy-start.18 = (bf16[2,512,256]{2,1,0:T(8,128)(2,1)}, bf16[2,512,256]{2,1,0:T(8,128)(2,1)S(1)}, u32[]{:S(2)}) copy-start(bf16[2,512,256]{2,1,0:T(8,128)(2,1)S(1)} %collective-permute-done.2.far_core_ref) | copy-start | bytes 1572868
  32.2 49.3 %all-to-all-start.1 = ((bf16[8,2,2,32,256]{4,3,2,1,0:T(8,128)(2,1)}), bf16[8,2,2,32,256]{4,3,2,1,0:T(8,128)(2,1)}, u32[]{:S(2)}, u32[]{:S(2)}) async-start(bf16[8,2,2,32,256]{4,3,2,1,0:T(8,128)(2,1)} %pick_new.1), calls=%async_computation.1 | async-start | bytes 1048576 | tf_op jit(solution)/shard_map/all_to_all | solution.py:435
  37.7 6.5 %collective-permute-start.3 = (bf16[16,2,32,256]{3,2,1,0:T(8,128)(2,1)S(1)}, bf16[16,2,32,256]{3,2,1,0:T(8,128)(2,1)}, u32[]{:S(2)}, u32[]{:S(2)}) collective-permute-start(bf16[16,2,32,256]{3,2,1,0:T(8,128)(2,1)S(1)} %bitcast.14), channel_id=1, source_target_pairs={{0,1},{1,0},{2,3},{3,2},{4,5},{5,4},{6,7},{7,6},{8,9},{9,8},{10,11... | collective-permute-start | bytes 1572872 | tf_op jit(solution)/shard_map/ppermute | solution.py:431
  43.0 38.5 %collective-permute-start.5 = (bf16[16,2,32,256]{3,2,1,0:T(8,128)(2,1)}, bf16[16,2,32,256]{3,2,1,0:T(8,128)(2,1)}, u32[]{:S(2)}, u32[]{:S(2)}) collective-permute-start(bf16[16,2,32,256]{3,2,1,0:T(8,128)(2,1)} %collective-permute-done.4.far_ref), channel_id=1, source_target_pairs={{0,1},{1,0},{2,3},{3,2},{4,5},{5,4},{6,7},{7,6},{8,9},{9,8},{10,11... | collective-permute-start | bytes 1572872 | tf_op jit(solution)/shard_map/ppermute | solution.py:432
  44.2 1.0 copy-start.11
  45.2 1.0 copy-start.13
  46.2 1.0 copy-start.15
  47.3 1.0 copy-start.17
  48.3 1.0 copy-start.19
  76.2 2.3 %copy-start = (f32[10,512,256]{2,1,0:T(8,128)}, f32[10,512,256]{2,1,0:T(8,128)S(1)}, u32[]{:S(2)}) copy-start(f32[10,512,256]{2,1,0:T(8,128)S(1)} %get-tuple-element.11.acc_ref) | copy-start | bytes 15728644
  78.5 1.5 %copy-start.2 = (f32[10,512,128]{2,1,0:T(8,128)}, f32[10,512,128]{2,1,0:T(8,128)S(1)}, u32[]{:S(2)}) copy-start(f32[10,512,128]{2,1,0:T(8,128)S(1)} %get-tuple-element.12.max_ref) | copy-start | bytes 7864324
  80.0 1.5 %copy-start.4 = (f32[10,512,128]{2,1,0:T(8,128)}, f32[10,512,128]{2,1,0:T(8,128)S(1)}, u32[]{:S(2)}) copy-start(f32[10,512,128]{2,1,0:T(8,128)S(1)} %get-tuple-element.13.sum_ref) | copy-start | bytes 7864324
  81.5 2.5 %copy-start.1 = (f32[10,512,256]{2,1,0:T(8,128)S(1)}, f32[10,512,256]{2,1,0:T(8,128)}, u32[]{:S(2)}) copy-start(f32[10,512,256]{2,1,0:T(8,128)} %copy-done) | copy-start | bytes 15728644
  84.0 1.7 %copy-start.3 = (f32[10,512,128]{2,1,0:T(8,128)S(1)}, f32[10,512,128]{2,1,0:T(8,128)}, u32[]{:S(2)}) copy-start(f32[10,512,128]{2,1,0:T(8,128)} %copy-done.2) | copy-start | bytes 7864324
  85.7 1.7 %copy-start.5 = (f32[10,512,128]{2,1,0:T(8,128)S(1)}, f32[10,512,128]{2,1,0:T(8,128)}, u32[]{:S(2)}) copy-start(f32[10,512,128]{2,1,0:T(8,128)} %copy-done.4) | copy-start | bytes 7864324
  87.5 1.1 copy-start.7
  88.6 1.1 copy-start.9
